TPU v7x, 32 devices: a whole 2x2x4 slice. The times are simulated.
32 devices in a mesh: groups: 2 (over x), dom: 8 (over z, y), mp: 2 (over core).
Axes of the slice: x: 2, y: 2, z: 4, core: 2. Of those that a mesh axis runs over, the one named last changes fastest.
Arguments:
- feats: bfloat16 [24576, 256], P(('groups', 'dom')), parts along dimension 0, may hold values from -6 to 6
- cell_count: int32 [16], P(('groups', 'dom')), parts along dimension 0, may hold values from 1 to 1536, 9216 in all
- tile_col: int32 [192, 8], P(('groups', 'dom')), parts along dimension 0, may hold values from 0 to 11, all different within a row
- tile_val: bfloat16 [192, 8, 128, 128], P(('groups', 'dom')), parts along dimension 0, may hold values from -0.1875 to 0.1875
- send_list: int32 [16, 8, 64], P(('groups', 'dom')), parts along dimension 0, may hold values from 0 to 1535
- send_count: int32 [16, 8], P(('groups', 'dom')), parts along dimension 0, may hold values from 1 to 64, 256 in all within a row
- recv_list: int32 [16, 8, 64], P(('groups', 'dom')), parts along dimension 0, may hold values from 0 to 1535
- gate_weight_matrix: bfloat16 [2, 256, 512], P(None, None, 'mp'), may hold values from -0.375 to 0.375
- w_up: bfloat16 [2, 256, 512], P(None, None, 'mp'), may hold values from -0.375 to 0.375
- w_down: bfloat16 [2, 512, 256], P(None, 'mp'), may hold values from -0.25 to 0.25
- out_grad: bfloat16 [24576, 256], P(('groups', 'dom')), parts along dimension 0, may hold values from -6 to 6
Outputs:
- final: bfloat16 [24576, 256], P(('groups', 'dom')), parts along dimension 0
- feat_grad: float32 [24576, 256], P(('groups', 'dom')), parts along dimension 0
- grad_gate: float32 [4, 256, 512], P('groups', None, 'mp'), parts along dimension 0
- grad_up: float32 [4, 256, 512], P('groups', None, 'mp'), parts along dimension 0
- down_weight_gradient: float32 [4, 512, 256], P('groups', 'mp'), parts along dimension 0
There are 2 independent parts, one for each index of `groups`. A program takes and returns all parts, laid end to end along the dimension named above; an argument that names none is the same for every part. Nothing has to cross between parts.
Inputs may be any that keep to these rules, and one draw needn't show every extreme that they name: Partition p has live cells in its rows 0 to cell_count[p] - 1; some partition is full in every draw, and the counts sum to 9216. `tile_col`: the entries of one row block are distinct local block columns; every block column is named somewhere. `send_list`: slots at or past send_count are unused. `send_count`: entry [s, q] counts live slots from partition s to partition q, its own included; each row sums to 256 and its largest entry is exactly 64. `recv_list`: entry [q, s, k] is the receiver's local row fed by slot k from partition s.
All inputs are finite; a program needn't handle non-finite values. No bound on the sum of `cell_count` on one device may be relied on, other than what follows from the above.
Results may differ from a plain program's by a relative error of at most 0.03.
Values may be sent and summed in bfloat16 or wider, within the bound.
A program may use at most 128 MiB of HBM per device.

v0:
```python
import functools

import jax
import jax.numpy as jnp
from jax import lax
from jax.experimental import pallas as pl
from jax.experimental.pallas import tpu as pltpu
from jax.sharding import PartitionSpec as P

MESH = pl.DeviceIdType.MESH
BLOCK = 128
LANES = 128
TILE = 256


def dot_nn(left, right):
    return lax.dot_general(
        left, right, (((1,), (0,)), ((), ())), preferred_element_type=jnp.float32
    )


def dot_nt(left, right):
    return lax.dot_general(
        left, right, (((1,), (1,)), ((), ())), preferred_element_type=jnp.float32
    )


def dot_tn(left, right):
    return lax.dot_general(
        left, right, (((0,), (0,)), ((), ())), preferred_element_type=jnp.float32
    )


def remote(src, dst, send_sem, recv_sem, dom, core):
    return pltpu.make_async_remote_copy(
        src_ref=src,
        dst_ref=dst,
        send_sem=send_sem,
        recv_sem=recv_sem,
        device_id={"dom": dom, "mp": core},
        device_id_type=MESH,
    )


def aligned(index, size):
    return pl.ds(pl.multiple_of(index * size, size), size)


def kernel(
    parts,
    inv_ref,
    count_ref,
    idx_ref,
    feats_ref,
    tiles_ref,
    cot_ref,
    wg_in,
    wu_in,
    wd_in,
    final_ref,
    fg_ref,
    gg_out,
    gu_out,
    gd_out,
    adj,
    adj_t,
    own_pick,
    s_t,
    r_t,
    states,
    acts,
    hid,
    pre_g,
    pre_u,
    down_in,
    agg_grad,
    wg,
    wu,
    wd,
    sbuf,
    halo,
    grads,
    res,
    p_one,
    p_sum,
    p_two,
    q_one,
    q_sum,
    q_two,
    h_send,
    h_recv,
    f_send,
    f_recv,
    w_send,
    w_recv,
    a_send,
    a_recv,
):
    me = lax.axis_index("dom")
    core = lax.axis_index("mp")
    sib = 1 - core
    layers = wg_in.shape[0]
    width = feats_ref.shape[1]
    units = wg_in.shape[2]
    rows = feats_ref.shape[0]
    blocks = rows // BLOCK
    tiles = rows // TILE
    slots = sbuf.shape[2]
    outer = parts // 2
    y = lax.rem(me, 2)
    z = me // 2
    f32, bf16 = jnp.float32, jnp.bfloat16

    barrier = pltpu.get_barrier_semaphore()

    def greet(i, _):
        q = lax.rem(me + i, parts)
        pl.semaphore_signal(
            barrier, inc=1, device_id={"dom": q, "mp": core}, device_id_type=MESH
        )
        return 0

    lax.fori_loop(1, parts, greet, 0)
    pl.semaphore_signal(barrier, inc=1, device_id={"dom": me, "mp": sib}, device_id_type=MESH)

    count = count_ref[0]

    def mask_of(i):
        index = lax.broadcasted_iota(jnp.int32, (TILE, 1), 0) + i * TILE
        return (index < count).astype(f32)

    def mask_rows(i, _):
        at = aligned(i, TILE)
        states[0, at, :] = (feats_ref[at, :].astype(f32) * mask_of(i)).astype(bf16)
        return 0

    lax.fori_loop(0, tiles, mask_rows, 0)

    columns = jnp.transpose(idx_ref[...])
    own_rows = parts * slots
    own_cols = jnp.where(core == 0, columns[:own_rows], columns[own_rows:])
    step = min(own_rows, TILE)
    for begin in range(0, own_rows, step):
        lane = lax.broadcasted_iota(jnp.int32, (step, rows), 1)
        own_pick[begin : begin + step, :] = (own_cols[begin : begin + step, 0:1] == lane).astype(
            f32
        ).astype(bf16)

    pl.semaphore_wait(barrier, parts)

    def halo_send(phase, onehot, source):
        for begin in range(0, own_rows, step):
            picked = dot_nn(onehot[begin : begin + step, :], source[...]).astype(bf16)
            sbuf[phase, begin // slots : (begin + step) // slots] = picked.reshape(
                step // slots, slots, width
            )
        halo[phase, core, me] = sbuf[phase, me]

        def send(i, _):
            q = lax.rem(me + i, parts)
            remote(
                sbuf.at[phase, q],
                halo.at[phase, core, me],
                h_send.at[phase, q],
                h_recv.at[phase, me],
                q,
                core,
            ).start()
            return 0

        lax.fori_loop(1, parts, send, 0)
        forward(phase, me).start()

    def forward(phase, s):
        return remote(
            halo.at[phase, core, s],
            halo.at[phase, core, s],
            f_send.at[phase, s],
            f_recv.at[phase, s],
            me,
            sib,
        )

    def arrival(phase, s):
        return remote(
            sbuf.at[phase, s],
            halo.at[phase, core, s],
            h_send.at[phase, s],
            h_recv.at[phase, s],
            s,
            core,
        )

    def halo_recv(phase):
        def take(i, _):
            s = lax.rem(me + parts - i, parts)
            arrival(phase, s).wait_recv()
            forward(phase, s).start()
            return 0

        lax.fori_loop(1, parts, take, 0)

        def settle(s, _):
            remote(
                halo.at[phase, sib, s],
                halo.at[phase, sib, s],
                f_send.at[phase, s],
                f_recv.at[phase, s],
                me,
                sib,
            ).wait_recv()
            return 0

        lax.fori_loop(0, parts, settle, 0)

    def landed_rows(phase):
        return halo[phase].reshape(2 * own_rows, width)

    halo_send(0, own_pick, states.at[0])

    weight_copies = []
    for k, (src, dst) in enumerate(((wg_in, wg), (wu_in, wu), (wd_in, wd))):
        copy = remote(src, dst.at[core], w_send.at[k], w_recv.at[k], me, sib)
        copy.start()
        weight_copies.append(copy)
        dst[core] = src[...]

    def build(r, _):
        for c in range(blocks):
            j = inv_ref[r, c]
            tile = tiles_ref[r, jnp.maximum(j, 0)]
            adj[aligned(r, BLOCK), c * BLOCK : (c + 1) * BLOCK] = jnp.where(
                j >= 0, tile, jnp.zeros_like(tile)
            )
        return 0

    lax.fori_loop(0, blocks, build, 0)

    def build_columns(i, _):
        at = aligned(i, TILE)
        index = lax.broadcasted_iota(jnp.int32, (TILE, 2 * own_rows), 0) + i * TILE
        s_t[at, :] = (idx_ref[0:1, :] == index).astype(f32).astype(bf16)
        r_t[at, :] = (idx_ref[1:2, :] == index).astype(f32).astype(bf16)
        return 0

    def build_back():
        for begin in range(0, own_rows, step):
            lane = lax.broadcasted_iota(jnp.int32, (step, rows), 1)
            own_pick[begin : begin + step, :] = (own_cols[begin : begin + step, 1:2] == lane).astype(
                f32
            ).astype(bf16)

    def turn_tiles():
        def turn(r, _):
            for c in range(blocks):
                adj_t[c * BLOCK : (c + 1) * BLOCK, aligned(r, BLOCK)] = jnp.transpose(
                    adj[aligned(r, BLOCK), c * BLOCK : (c + 1) * BLOCK]
                )
            return 0

        lax.fori_loop(0, blocks, turn, 0)

    for layer in range(layers):
        if layer:
            halo_send(layer, own_pick, states.at[layer])
        state = states.at[layer]

        def gather(i, _, state=state):
            at = aligned(i, TILE)
            fg_ref[at, :] = dot_nn(adj[at, :], state[...])
            return 0

        lax.fori_loop(0, tiles, gather, 0)
        if layer == 0:
            lax.fori_loop(0, tiles, build_columns, 0)
            turn_tiles()
            for copy in weight_copies:
                copy.wait_recv()
        if layer == layers - 1:
            build_back()
        halo_recv(layer)

        def mlp(i, _, layer=layer, state=state):
            at = aligned(i, TILE)
            act = (fg_ref[at, :] + dot_nn(r_t[at, :], landed_rows(layer))).astype(bf16)
            acts[layer, at, :] = act
            mixed = jnp.zeros((TILE, width), f32)
            for h in range(2):
                gate = dot_nn(act, wg[h, layer])
                up = dot_nn(act, wu[h, layer])
                sg = 0.5 * jnp.tanh(0.5 * gate) + 0.5
                silu = gate * sg
                hidden = (silu * up).astype(bf16)
                hid[layer, h, at, :] = hidden
                pre_g[layer, h, at, :] = (up * (sg * (1.0 + gate * (1.0 - sg)))).astype(bf16)
                pre_u[layer, h, at, :] = silu.astype(bf16)
                mixed = mixed + dot_nn(hidden, wd[h, layer])
            new = ((state[at, :].astype(f32) + mixed) * mask_of(i)).astype(bf16)
            if layer + 1 < layers:
                states[layer + 1, at, :] = new
            else:
                final_ref[at, :] = new
            return 0

        lax.fori_loop(0, tiles, mlp, 0)

    total = grads.shape[1]
    p_rows = total * 2 // 3
    p_half = p_rows // 2
    p_seg = p_half // outer
    q_seg = (total - p_rows) // outer
    q_half = q_seg // 2

    def at_rows(base, index, size):
        return pl.ds(pl.multiple_of(base + index * size, 16), size)

    def each_other(fn):
        def go(i, _):
            fn(lax.rem(z + i, outer))
            return 0

        lax.fori_loop(1, outer, go, 0)

    def pair(stage, layer, src, dst):
        return remote(
            src,
            dst,
            a_send.at[layer, stage, outer],
            a_recv.at[layer, stage, outer],
            z * 2 + 1 - y,
            core,
        )

    def line(stage, layer, src, dst, to, slot):
        return remote(
            src,
            dst,
            a_send.at[layer, stage, to],
            a_recv.at[layer, stage, slot],
            to * 2 + y,
            core,
        )

    def reduce_one(layer):
        pair(0, layer, grads.at[layer, at_rows(0, 1 - y, p_half)], p_one.at[layer]).start()
        each_other(
            lambda t: line(
                0,
                layer,
                grads.at[layer, at_rows(p_rows, t, q_seg)],
                q_one.at[layer, z],
                t,
                z,
            ).start()
        )
        q_one[layer, z] = grads[layer, at_rows(p_rows, z, q_seg)]

    def reduce_two(layer):
        pair(0, layer, grads.at[layer, at_rows(0, 1 - y, p_half)], p_one.at[layer]).wait_recv()
        p_sum[layer] = (
            grads[layer, at_rows(0, y, p_half)].astype(f32) + p_one[layer].astype(f32)
        ).astype(bf16)
        each_other(
            lambda t: line(
                1, layer, p_sum.at[layer, at_rows(0, t, p_seg)], p_two.at[layer, z], t, z
            ).start()
        )
        p_two[layer, z] = p_sum[layer, at_rows(0, z, p_seg)]
        each_other(
            lambda t: line(
                0,
                layer,
                grads.at[layer, at_rows(p_rows, t, q_seg)],
                q_one.at[layer, t],
                t,
                t,
            ).wait_recv()
        )
        q_sum[layer] = jnp.sum(q_one[layer].astype(f32), axis=0).astype(bf16)
        pair(1, layer, q_sum.at[layer, at_rows(0, 1 - y, q_half)], q_two.at[layer]).start()

    def reduce_three(layer):
        each_other(
            lambda t: line(
                1, layer, p_sum.at[layer, at_rows(0, t, p_seg)], p_two.at[layer, t], t, t
            ).wait_recv()
        )
        mine = at_rows(y * p_half, z, p_seg)
        res[layer, mine] = jnp.sum(p_two[layer].astype(f32), axis=0).astype(bf16)
        each_other(
            lambda t: line(2, layer, res.at[layer, mine], res.at[layer, mine], t, z).start()
        )
        pair(1, layer, q_sum.at[layer, at_rows(0, 1 - y, q_half)], q_two.at[layer]).wait_recv()
        own = at_rows(p_rows + z * q_seg, y, q_half)
        res[layer, own] = (
            q_sum[layer, at_rows(0, y, q_half)].astype(f32) + q_two[layer].astype(f32)
        ).astype(bf16)
        pair(2, layer, res.at[layer, own], res.at[layer, own]).start()

    def reduce_four(layer):
        def landed(t):
            there = at_rows(y * p_half, t, p_seg)
            line(2, layer, res.at[layer, there], res.at[layer, there], t, t).wait_recv()

        each_other(landed)
        half = at_rows(0, y, p_half)
        pair(3, layer, res.at[layer, half], res.at[layer, half]).start()
        other = at_rows(p_rows + z * q_seg, 1 - y, q_half)
        pair(2, layer, res.at[layer, other], res.at[layer, other]).wait_recv()
        own = at_rows(p_rows, z, q_seg)
        each_other(lambda t: line(3, layer, res.at[layer, own], res.at[layer, own], t, z).start())

    def reduce_end(layer):
        half = at_rows(0, 1 - y, p_half)
        pair(3, layer, res.at[layer, half], res.at[layer, half]).wait_recv()

        def landed(t):
            there = at_rows(p_rows, t, q_seg)
            line(3, layer, res.at[layer, there], res.at[layer, there], t, t).wait_recv()

        each_other(landed)
        at = 0
        for out in (gg_out, gu_out, gd_out):
            height, wide = out.shape[1:]
            for c in range(0, wide, LANES):
                out[layer, :, c : c + LANES] = res[layer, at : at + height].astype(f32)
                at += height

    def reduce_drain(layer):
        pair(0, layer, grads.at[layer, at_rows(0, 1 - y, p_half)], p_one.at[layer]).wait_send()
        pair(1, layer, q_sum.at[layer, at_rows(0, 1 - y, q_half)], q_two.at[layer]).wait_send()
        own = at_rows(p_rows + z * q_seg, y, q_half)
        pair(2, layer, res.at[layer, own], res.at[layer, own]).wait_send()
        half = at_rows(0, y, p_half)
        pair(3, layer, res.at[layer, half], res.at[layer, half]).wait_send()
        mine = at_rows(y * p_half, z, p_seg)
        whole = at_rows(p_rows, z, q_seg)

        def sent(t):
            line(
                0,
                layer,
                grads.at[layer, at_rows(p_rows, t, q_seg)],
                q_one.at[layer, z],
                t,
                z,
            ).wait_send()
            line(
                1, layer, p_sum.at[layer, at_rows(0, t, p_seg)], p_two.at[layer, z], t, z
            ).wait_send()
            line(2, layer, res.at[layer, mine], res.at[layer, mine], t, z).wait_send()
            line(3, layer, res.at[layer, whole], res.at[layer, whole], t, z).wait_send()

        each_other(sent)

    def start_rows(i, _):
        at = aligned(i, TILE)
        fg_ref[at, :] = cot_ref[at, :].astype(f32) * mask_of(i)
        return 0

    lax.fori_loop(0, tiles, start_rows, 0)

    for layer in reversed(range(layers)):
        phase = 2 * layers - 1 - layer
        last = layer == layers - 1

        def mlp_back(i, _, layer=layer):
            at = aligned(i, TILE)
            down = fg_ref[at, :].astype(bf16)
            down_in[at, :] = down
            total = jnp.zeros((TILE, width), f32)
            for h in range(2):
                hidden_grad = dot_nt(down, wd[h, layer])
                gate_grad = (hidden_grad * pre_g[layer, h, at, :].astype(f32)).astype(bf16)
                up_grad = (hidden_grad * pre_u[layer, h, at, :].astype(f32)).astype(bf16)
                pre_g[layer, h, at, :] = gate_grad
                pre_u[layer, h, at, :] = up_grad
                total = total + dot_nt(gate_grad, wg[h, layer]) + dot_nt(up_grad, wu[h, layer])
            agg_grad[at, :] = total.astype(bf16)
            return 0

        lax.fori_loop(0, tiles, mlp_back, 0)
        halo_send(phase, own_pick, agg_grad)
        if not last:
            reduce_three(layer + 1)

        at = 0
        act = acts[layer]
        for left, right in (
            (act, pre_g[layer, core]),
            (act, pre_u[layer, core]),
            (hid[layer, core], down_in[...]),
        ):
            part = dot_tn(left, right).astype(bf16)
            for c in range(0, part.shape[1], LANES):
                grads[layer, at : at + part.shape[0], :] = part[:, c : c + LANES]
                at += part.shape[0]
        reduce_one(layer)

        def gather_back(i, _):
            at = aligned(i, TILE)
            fg_ref[at, :] = fg_ref[at, :] + dot_nn(adj_t[at, :], agg_grad[...])
            return 0

        lax.fori_loop(0, tiles, gather_back, 0)
        if not last:
            reduce_four(layer + 1)
        halo_recv(phase)

        def finish(i, _, phase=phase):
            at = aligned(i, TILE)
            fg_ref[at, :] = (fg_ref[at, :] + dot_nn(s_t[at, :], landed_rows(phase))) * mask_of(i)
            return 0

        if last:
            lax.fori_loop(0, tiles, finish, 0)
            reduce_two(layer)
        else:
            reduce_two(layer)
            lax.fori_loop(0, tiles, finish, 0)
            reduce_end(layer + 1)

    reduce_three(0)
    reduce_four(0)
    reduce_end(0)
    for layer in range(layers):
        reduce_drain(layer)
    for copy in weight_copies:
        copy.wait_send()
    for phase in range(2 * layers):

        def drained(i, _, phase=phase):
            q = lax.rem(me + i, parts)
            arrival(phase, q).wait_send()
            forward(phase, q).wait_send()
            return 0

        lax.fori_loop(1, parts, drained, 0)
        forward(phase, me).wait_send()


def local(
    parts,
    feats,
    cell_count,
    tile_col,
    tile_val,
    send_list,
    send_count,
    recv_list,
    gate_weight_matrix,
    w_up,
    w_down,
    out_grad,
):
    rows, width = feats.shape
    layers, _, units = gate_weight_matrix.shape
    blocks, per_row = tile_col.shape
    slot_count = send_list.shape[2]
    half = slot_count // 2
    outer = parts // 2
    all_slots = parts * slot_count
    position = jnp.arange(1, per_row + 1, dtype=jnp.int32)[None, :, None]
    chosen = tile_col[:, :, None] == jnp.arange(blocks, dtype=jnp.int32)[None, None, :]
    inverse = jnp.sum(jnp.where(chosen, position, 0), axis=1) - 1
    live = jnp.arange(slot_count)[None, :] < send_count[0][:, None]
    listed = jnp.stack([jnp.where(live, send_list[0], -1), recv_list[0]])
    listed = jnp.swapaxes(listed.reshape(2, parts, 2, half), 1, 2).reshape(2, all_slots)
    listed = jnp.pad(listed, ((0, 6), (0, 0)))

    total = 2 * width * (units // LANES) + units * (width // LANES)
    p_half = total // 3
    q_seg = (total - 2 * p_half) // outer
    f32, bf16 = jnp.float32, jnp.bfloat16
    vmem = pl.BlockSpec(memory_space=pltpu.VMEM)
    smem = pl.BlockSpec(memory_space=pltpu.SMEM)
    phases = 2 * layers
    dma = pltpu.SemaphoreType.DMA
    return pl.pallas_call(
        functools.partial(kernel, parts),
        out_shape=(
            jax.ShapeDtypeStruct((rows, width), bf16),
            jax.ShapeDtypeStruct((rows, width), f32),
            jax.ShapeDtypeStruct((layers, width, units), f32),
            jax.ShapeDtypeStruct((layers, width, units), f32),
            jax.ShapeDtypeStruct((layers, units, width), f32),
        ),
        in_specs=[smem, smem] + [vmem] * 7,
        out_specs=[vmem] * 5,
        scratch_shapes=[
            pltpu.VMEM((rows, rows), bf16),
            pltpu.VMEM((rows, rows), bf16),
            pltpu.VMEM((all_slots // 2, rows), bf16),
            pltpu.VMEM((rows, all_slots), bf16),
            pltpu.VMEM((rows, all_slots), bf16),
            pltpu.VMEM((layers, rows, width), bf16),
            pltpu.VMEM((layers, rows, width), bf16),
            pltpu.VMEM((layers, 2, rows, units), bf16),
            pltpu.VMEM((layers, 2, rows, units), bf16),
            pltpu.VMEM((layers, 2, rows, units), bf16),
            pltpu.VMEM((rows, width), bf16),
            pltpu.VMEM((rows, width), bf16),
            pltpu.VMEM((2, layers, width, units), bf16),
            pltpu.VMEM((2, layers, width, units), bf16),
            pltpu.VMEM((2, layers, units, width), bf16),
            pltpu.VMEM((phases, parts, half, width), bf16),
            pltpu.VMEM((phases, 2, parts, half, width), bf16),
            pltpu.VMEM((layers, total, LANES), bf16),
            pltpu.VMEM((layers, total, LANES), bf16),
            pltpu.VMEM((layers, p_half, LANES), bf16),
            pltpu.VMEM((layers, p_half, LANES), bf16),
            pltpu.VMEM((layers, outer, p_half // outer, LANES), bf16),
            pltpu.VMEM((layers, outer, q_seg, LANES), bf16),
            pltpu.VMEM((layers, q_seg, LANES), bf16),
            pltpu.VMEM((layers, q_seg // 2, LANES), bf16),
            dma((phases, parts)),
            dma((phases, parts)),
            dma((phases, parts)),
            dma((phases, parts)),
            dma((3,)),
            dma((3,)),
            dma((layers, 4, outer + 1)),
            dma((layers, 4, outer + 1)),
        ],
        compiler_params=pltpu.CompilerParams(
            collective_id=0, has_side_effects=True, vmem_limit_bytes=60 * 1024 * 1024
        ),
        cost_estimate=pl.CostEstimate(
            flops=14 * 10**9, bytes_accessed=12 * 10**6, transcendentals=rows * units * 4
        ),
    )(
        inverse,
        cell_count,
        listed,
        feats,
        tile_val,
        out_grad,
        gate_weight_matrix,
        w_up,
        w_down,
    )


def solution(mesh):
    return jax.shard_map(
        functools.partial(local, mesh.shape["dom"]),
        mesh=mesh,
        in_specs=(
            P(("groups", "dom"), None),
            P(("groups", "dom")),
            P(("groups", "dom"), None),
            P(("groups", "dom"), None, None, None),
            P(("groups", "dom"), None, None),
            P(("groups", "dom"), None),
            P(("groups", "dom"), None, None),
            P(None, None, "mp"),
            P(None, None, "mp"),
            P(None, "mp", None),
            P(("groups", "dom"), None),
        ),
        out_specs=(
            P(("groups", "dom"), None),
            P(("groups", "dom"), None),
            P("groups", None, "mp"),
            P("groups", None, "mp"),
            P("groups", "mp", None),
        ),
        check_vma=False,
    )
```

profile of v0, /device:TPU:0, one launch (start us, length us, event | category | flops | bytes accessed | tf_op | source)
XLA Modules:
  0.0 88.5 jit_solution(12762383376029665698)
XLA Ops:
  1.3 0.8 fusion
  2.0 0.1 stack.8
  2.1 0.8 copy.19
  2.9 0.1 select_reduce_fusion
  3.0 0.6 broadcast_add_fusion.inv_ref
  3.6 0.8 stack.9
  4.4 0.1 reshape.56
  4.5 0.6 pad.4.idx_ref
  5.1 77.4 %shard_map.149 = (bf16[1536,256]{1,0:T(8,128)(2,1)}, f32[1536,256]{1,0:T(8,128)}, f32[2,256,256]{2,1,0:T(8,128)}, f32[2,256,256]{2,1,0:T(8,128)}, f32[2,256,256]{2,1,0:T(8,128)}) custom-call(s32[12,12]{1,0:T(8,128)} %broadcast_add_fusion.inv_ref, s32[1]{0:T(128)S(6)} %copy.27.count_ref, s32[8,512]{1,0:T(8,128)} %pad.4.idx_ref, bf16[1536,256]{1,0:T(8,128)(2,1)} %feats_ref.1, ...), custom_call_target="tpu_custom_call" | custom-call | flops 14000000000 | bytes 12000000 | tf_op jit(solution)/shard_map/pallas_call | solution.py:579
  82.5 0.0 copy-start
  82.5 2.2 %copy.28 = bf16[1536,256]{1,0:T(8,128)(2,1)} copy(bf16[1536,256]{1,0:T(8,128)(2,1)} %get-tuple-element.10) | data formatting | bytes 1572864
  84.7 0.0 copy-done
  84.7 0.0 copy-start.3
  84.7 0.0 copy-start.2
  84.7 1.1 %copy.29 = f32[1536,256]{1,0:T(8,128)} copy(f32[1536,256]{1,0:T(8,128)S(1)} %copy-done) | data formatting | bytes 3145728
  85.8 0.2 copy-done.3
  86.1 0.0 copy-start.1
  86.1 0.8 copy.30
  86.9 0.0 copy-done.2
  86.9 0.8 copy.31
  87.7 0.0 copy-done.1
  87.7 0.8 copy.32
  (4 shorter events, 0.0 us)
Async XLA Ops:
  82.5 2.2 %copy-start = (f32[1536,256]{1,0:T(8,128)S(1)}, f32[1536,256]{1,0:T(8,128)}, u32[]{:S(2)}) copy-start(f32[1536,256]{1,0:T(8,128)} %get-tuple-element.11) | copy-start | bytes 4718596
  84.7 1.4 %copy-start.3 = (f32[2,256,256]{2,1,0:T(8,128)S(1)}, f32[2,256,256]{2,1,0:T(8,128)}, u32[]{:S(2)}) copy-start(f32[2,256,256]{2,1,0:T(8,128)} %get-tuple-element.12) | copy-start | bytes 1572868
  84.7 2.2 %copy-start.2 = (f32[2,256,256]{2,1,0:T(8,128)S(1)}, f32[2,256,256]{2,1,0:T(8,128)}, u32[]{:S(2)}) copy-start(f32[2,256,256]{2,1,0:T(8,128)} %get-tuple-element.13) | copy-start | bytes 1572868
  86.1 1.6 %copy-start.1 = (f32[2,256,256]{2,1,0:T(8,128)S(1)}, f32[2,256,256]{2,1,0:T(8,128)}, u32[]{:S(2)}) copy-start(f32[2,256,256]{2,1,0:T(8,128)} %get-tuple-element.14) | copy-start | bytes 1572868
where the time goes:
time: 88.7 us; the launch traced here: 88.5 us
  Pallas kernels  77.4 us (87%)
  local copies, waits for them, and re-layouts  8.26 us (9%)
  other arithmetic  1.47 us (2%)
  between operations  1.32 us (1%)
    pallas_call x1, Pallas kernels, local(): pl.pallas_call(functools.partial(kernel, parts), out_shape=(jax.ShapeDtyp...  77.4 us
    unnamed x14, local copies, waits for them, and re-layouts  6.71 us

commit v1 on v0

--- a/solution.py
+++ b/solution.py
@@ -43,6 +43,8 @@
 
 
 def aligned(index, size):
+    if isinstance(index, int):
+        return pl.ds(index * size, size)
     return pl.ds(pl.multiple_of(index * size, size), size)
 
 
@@ -72,8 +74,6 @@
     hid,
     pre_g,
     pre_u,
-    down_in,
-    agg_grad,
     wg,
     wu,
     wd,
@@ -111,6 +111,10 @@
     z = me // 2
     f32, bf16 = jnp.float32, jnp.bfloat16
 
+    def each_tile(body):
+        for i in range(tiles):
+            body(i, 0)
+
     barrier = pltpu.get_barrier_semaphore()
 
     def greet(i, _):
@@ -134,7 +138,7 @@
         states[0, at, :] = (feats_ref[at, :].astype(f32) * mask_of(i)).astype(bf16)
         return 0
 
-    lax.fori_loop(0, tiles, mask_rows, 0)
+    each_tile(mask_rows)
 
     columns = jnp.transpose(idx_ref[...])
     own_rows = parts * slots
@@ -236,10 +240,15 @@
 
     lax.fori_loop(0, blocks, build, 0)
 
-    def build_columns(i, _):
+    def build_send(i, _):
         at = aligned(i, TILE)
         index = lax.broadcasted_iota(jnp.int32, (TILE, 2 * own_rows), 0) + i * TILE
         s_t[at, :] = (idx_ref[0:1, :] == index).astype(f32).astype(bf16)
+        return 0
+
+    def build_receive(i, _):
+        at = aligned(i, TILE)
+        index = lax.broadcasted_iota(jnp.int32, (TILE, 2 * own_rows), 0) + i * TILE
         r_t[at, :] = (idx_ref[1:2, :] == index).astype(f32).astype(bf16)
         return 0
 
@@ -265,19 +274,17 @@
             halo_send(layer, own_pick, states.at[layer])
         state = states.at[layer]
 
-        def gather(i, _, state=state):
-            at = aligned(i, TILE)
+        for begin in range(0, rows, 2 * TILE):
+            at = pl.ds(begin, 2 * TILE)
             fg_ref[at, :] = dot_nn(adj[at, :], state[...])
-            return 0
-
-        lax.fori_loop(0, tiles, gather, 0)
         if layer == 0:
-            lax.fori_loop(0, tiles, build_columns, 0)
-            turn_tiles()
+            each_tile(build_receive)
             for copy in weight_copies:
                 copy.wait_recv()
         if layer == layers - 1:
             build_back()
+            each_tile(build_send)
+            turn_tiles()
         halo_recv(layer)
 
         def mlp(i, _, layer=layer, state=state):
@@ -302,7 +309,7 @@
                 final_ref[at, :] = new
             return 0
 
-        lax.fori_loop(0, tiles, mlp, 0)
+        each_tile(mlp)
 
     total = grads.shape[1]
     p_rows = total * 2 // 3
@@ -453,12 +460,14 @@
 
         each_other(sent)
 
+    down_in, agg_grad = states.at[0], states.at[1]
+
     def start_rows(i, _):
         at = aligned(i, TILE)
         fg_ref[at, :] = cot_ref[at, :].astype(f32) * mask_of(i)
         return 0
 
-    lax.fori_loop(0, tiles, start_rows, 0)
+    each_tile(start_rows)
 
     for layer in reversed(range(layers)):
         phase = 2 * layers - 1 - layer
@@ -468,43 +477,56 @@
             at = aligned(i, TILE)
             down = fg_ref[at, :].astype(bf16)
             down_in[at, :] = down
-            total = jnp.zeros((TILE, width), f32)
             for h in range(2):
                 hidden_grad = dot_nt(down, wd[h, layer])
                 gate_grad = (hidden_grad * pre_g[layer, h, at, :].astype(f32)).astype(bf16)
                 up_grad = (hidden_grad * pre_u[layer, h, at, :].astype(f32)).astype(bf16)
                 pre_g[layer, h, at, :] = gate_grad
                 pre_u[layer, h, at, :] = up_grad
-                total = total + dot_nt(gate_grad, wg[h, layer]) + dot_nt(up_grad, wu[h, layer])
+            return 0
+
+        def through_weights(i, _, layer=layer):
+            at = aligned(i, TILE)
+            total = jnp.zeros((TILE, width), f32)
+            for h in range(2):
+                total = total + dot_nt(pre_g[layer, h, at, :], wg[h, layer])
+                total = total + dot_nt(pre_u[layer, h, at, :], wu[h, layer])
             agg_grad[at, :] = total.astype(bf16)
             return 0
 
-        lax.fori_loop(0, tiles, mlp_back, 0)
+        def weight_gradients(layer=layer):
+            at = 0
+            act = acts[layer]
+            for left, right in (
+                (act, pre_g[layer, core]),
+                (act, pre_u[layer, core]),
+                (hid[layer, core], down_in[...]),
+            ):
+                part = dot_tn(left, right).astype(bf16)
+                for c in range(0, part.shape[1], LANES):
+                    grads[layer, at : at + part.shape[0], :] = part[:, c : c + LANES]
+                    at += part.shape[0]
+            reduce_one(layer)
+
+        each_tile(mlp_back)
+        if layer == 0:
+            if not last:
+                reduce_three(layer + 1)
+            weight_gradients()
+        each_tile(through_weights)
         halo_send(phase, own_pick, agg_grad)
-        if not last:
-            reduce_three(layer + 1)
-
-        at = 0
-        act = acts[layer]
-        for left, right in (
-            (act, pre_g[layer, core]),
-            (act, pre_u[layer, core]),
-            (hid[layer, core], down_in[...]),
-        ):
-            part = dot_tn(left, right).astype(bf16)
-            for c in range(0, part.shape[1], LANES):
-                grads[layer, at : at + part.shape[0], :] = part[:, c : c + LANES]
-                at += part.shape[0]
-        reduce_one(layer)
-
-        def gather_back(i, _):
-            at = aligned(i, TILE)
-            fg_ref[at, :] = fg_ref[at, :] + dot_nn(adj_t[at, :], agg_grad[...])
-            return 0
-
-        lax.fori_loop(0, tiles, gather_back, 0)
+        if layer:
+            if not last:
+                reduce_three(layer + 1)
+            weight_gradients()
         if not last:
             reduce_four(layer + 1)
+
+        for begin in range(0, rows, 2 * TILE):
+            at = pl.ds(begin, 2 * TILE)
+            fg_ref[at, :] = fg_ref[at, :] + dot_nn(adj_t[at, :], agg_grad[...])
+        if not last:
+            reduce_two(layer)
         halo_recv(phase)
 
         def finish(i, _, phase=phase):
@@ -512,12 +534,10 @@
             fg_ref[at, :] = (fg_ref[at, :] + dot_nn(s_t[at, :], landed_rows(phase))) * mask_of(i)
             return 0
 
+        each_tile(finish)
         if last:
-            lax.fori_loop(0, tiles, finish, 0)
             reduce_two(layer)
         else:
-            reduce_two(layer)
-            lax.fori_loop(0, tiles, finish, 0)
             reduce_end(layer + 1)
 
     reduce_three(0)
@@ -537,6 +557,25 @@
 
         lax.fori_loop(1, parts, drained, 0)
         forward(phase, me).wait_send()
+
+
+def hand_over(*refs):
+    sems = refs[-1]
+    count = (len(refs) - 1) // 2
+    copies = []
+    for k in range(count):
+        source, target = refs[k], refs[count + k]
+        cuts = 2 if source.shape[0] < 8 else 4
+        size = source.shape[0] // cuts
+        for cut in range(cuts):
+            at = pl.ds(cut * size, size)
+            copies.append(
+                pltpu.make_async_copy(source.at[at], target.at[at], sems.at[k, cut])
+            )
+    for copy in copies:
+        copy.start()
+    for copy in copies:
+        copy.wait()
 
 
 def local(
@@ -576,7 +615,7 @@
     smem = pl.BlockSpec(memory_space=pltpu.SMEM)
     phases = 2 * layers
     dma = pltpu.SemaphoreType.DMA
-    return pl.pallas_call(
+    outs = pl.pallas_call(
         functools.partial(kernel, parts),
         out_shape=(
             jax.ShapeDtypeStruct((rows, width), bf16),
@@ -593,13 +632,11 @@
             pltpu.VMEM((all_slots // 2, rows), bf16),
             pltpu.VMEM((rows, all_slots), bf16),
             pltpu.VMEM((rows, all_slots), bf16),
-            pltpu.VMEM((layers, rows, width), bf16),
+            pltpu.VMEM((max(layers, 2), rows, width), bf16),
             pltpu.VMEM((layers, rows, width), bf16),
             pltpu.VMEM((layers, 2, rows, units), bf16),
             pltpu.VMEM((layers, 2, rows, units), bf16),
             pltpu.VMEM((layers, 2, rows, units), bf16),
-            pltpu.VMEM((rows, width), bf16),
-            pltpu.VMEM((rows, width), bf16),
             pltpu.VMEM((2, layers, width, units), bf16),
             pltpu.VMEM((2, layers, width, units), bf16),
             pltpu.VMEM((2, layers, units, width), bf16),
@@ -639,6 +676,13 @@
         w_up,
         w_down,
     )
+    return pl.pallas_call(
+        hand_over,
+        out_shape=tuple(jax.ShapeDtypeStruct(out.shape, out.dtype) for out in outs),
+        in_specs=[pl.BlockSpec(memory_space=pl.ANY)] * len(outs),
+        out_specs=[pl.BlockSpec(memory_space=pl.ANY)] * len(outs),
+        scratch_shapes=[dma((len(outs), 4))],
+    )(*outs)
 
 
 def solution(mesh):

time: 88.7 us -> 197 us (2.22)
  Pallas kernels: 77.4 us -> 191 us
  local copies, waits for them, and re-layouts: 8.26 us -> 2.32 us
    pallas_call x0 -> x1, Pallas kernels: none -> 120 us  [local(): pl.pallas_call(hand_over, out_shape=tuple((jax.ShapeDtypeStruct(out.shape...]
    pallas_call x1, Pallas kernels: 77.4 us -> 70.8 us  [local(): pl.pallas_call(functools.partial(kernel, parts), out_shape=(jax.ShapeDtyp...]
    unnamed x14 -> x1, local copies, waits for them, and re-layouts: 6.71 us -> 0.77 us
where the time goes in v1:
time: 197 us; the launch traced here: 196 us
  Pallas kernels  191 us (97%)
  local copies, waits for them, and re-layouts  2.32 us (1%)
    pallas_call x1, Pallas kernels, local(): pl.pallas_call(hand_over, out_shape=tuple((jax.ShapeDtypeStruct(out.shape...  120 us
    pallas_call x1, Pallas kernels, local(): pl.pallas_call(functools.partial(kernel, parts), out_shape=(jax.ShapeDtyp...  70.8 us

profile of v1, /device:TPU:0, one launch (start us, length us, event | category | flops | bytes accessed | tf_op | source)
XLA Modules:
  0.0 196.5 jit_solution(13480481257988738043)
XLA Ops:
  1.3 0.8 fusion
  2.0 0.1 stack.8
  2.1 0.8 copy.19
  2.9 0.1 select_reduce_fusion
  3.0 0.6 broadcast_add_fusion.inv_ref
  3.6 0.8 stack.9
  4.4 0.1 reshape.56
  4.5 0.6 pad.4.idx_ref
  5.1 70.8 %shard_map.149 = (bf16[1536,256]{1,0:T(8,128)(2,1)}, f32[1536,256]{1,0:T(8,128)}, f32[2,256,256]{2,1,0:T(8,128)}, f32[2,256,256]{2,1,0:T(8,128)}, f32[2,256,256]{2,1,0:T(8,128)}) custom-call(s32[12,12]{1,0:T(8,128)} %broadcast_add_fusion.inv_ref, s32[1]{0:T(128)S(6)} %copy.22.count_ref, s32[8,512]{1,0:T(8,128)} %pad.4.idx_ref, bf16[1536,256]{1,0:T(8,128)(2,1)} %feats_ref.1, ...), custom_call_target="tpu_custom_call" | custom-call | flops 14000000000 | bytes 12000000 | tf_op jit(solution)/shard_map/pallas_call | solution.py:618
  75.9 120.4 %shard_map.150 = (bf16[1536,256]{1,0:T(8,128)(2,1)}, f32[1536,256]{1,0:T(8,128)}, f32[2,256,256]{2,1,0:T(8,128)}, f32[2,256,256]{2,1,0:T(8,128)}, f32[2,256,256]{2,1,0:T(8,128)}) custom-call(bf16[1536,256]{1,0:T(8,128)(2,1)} %get-tuple-element.10.refs_0_, f32[1536,256]{1,0:T(8,128)} %get-tuple-element.11.refs_1_, f32[2,256,256]{2,1,0:T(8,128)} %get-tuple-element.12.refs_2_, ...), custom_call_target="tpu_custom_call" | custom-call | tf_op jit(solution)/shard_map/pallas_call | solution.py:679
  (4 shorter events, 0.0 us)

commit v2 on v1

--- a/solution.py
+++ b/solution.py
@@ -16,18 +16,6 @@
 def dot_nn(left, right):
     return lax.dot_general(
         left, right, (((1,), (0,)), ((), ())), preferred_element_type=jnp.float32
-    )
-
-
-def dot_nt(left, right):
-    return lax.dot_general(
-        left, right, (((1,), (1,)), ((), ())), preferred_element_type=jnp.float32
-    )
-
-
-def dot_tn(left, right):
-    return lax.dot_general(
-        left, right, (((0,), (0,)), ((), ())), preferred_element_type=jnp.float32
     )
 
 
@@ -50,33 +38,46 @@
 
 def kernel(
     parts,
-    inv_ref,
+    col_ref,
     count_ref,
-    idx_ref,
+    send_ref,
+    live_ref,
+    recv_ref,
     feats_ref,
-    tiles_ref,
-    cot_ref,
+    tiles_in,
+    cot_in,
     wg_in,
     wu_in,
     wd_in,
-    final_ref,
-    fg_ref,
+    final_out,
+    fg_out,
     gg_out,
     gu_out,
     gd_out,
+    idx_ref,
+    tiles_ref,
+    cot_ref,
+    final_ref,
+    fg_ref,
+    gg_ref,
+    gu_ref,
+    gd_ref,
     adj,
     adj_t,
     own_pick,
     s_t,
     r_t,
     states,
-    acts,
-    hid,
+    acts_t,
+    hid_t,
     pre_g,
     pre_u,
     wg,
     wu,
     wd,
+    wg_t,
+    wu_t,
+    wd_t,
     sbuf,
     halo,
     grads,
@@ -95,6 +96,8 @@
     w_recv,
     a_send,
     a_recv,
+    i_sem,
+    o_sem,
 ):
     me = lax.axis_index("dom")
     core = lax.axis_index("mp")
@@ -124,9 +127,19 @@
         )
         return 0
 
+    load_tiles = pltpu.make_async_copy(tiles_in, tiles_ref, i_sem.at[0])
+    load_cot = pltpu.make_async_copy(cot_in, cot_ref, i_sem.at[1])
+    load_weights = [
+        pltpu.make_async_copy(src, dst.at[core], i_sem.at[2 + k])
+        for k, (src, dst) in enumerate(((wg_in, wg), (wu_in, wu), (wd_in, wd)))
+    ]
     lax.fori_loop(1, parts, greet, 0)
     pl.semaphore_signal(barrier, inc=1, device_id={"dom": me, "mp": sib}, device_id_type=MESH)
 
+    for copy in load_weights:
+        copy.start()
+    load_tiles.start()
+    load_cot.start()
     count = count_ref[0]
 
     def mask_of(i):
@@ -140,16 +153,32 @@
 
     each_tile(mask_rows)
 
-    columns = jnp.transpose(idx_ref[...])
     own_rows = parts * slots
-    own_cols = jnp.where(core == 0, columns[:own_rows], columns[own_rows:])
     step = min(own_rows, TILE)
-    for begin in range(0, own_rows, step):
-        lane = lax.broadcasted_iota(jnp.int32, (step, rows), 1)
-        own_pick[begin : begin + step, :] = (own_cols[begin : begin + step, 0:1] == lane).astype(
-            f32
-        ).astype(bf16)
-
+    slot = lax.broadcasted_iota(jnp.int32, (2 * slots, parts), 0)
+    sources = jnp.where(slot < live_ref[...], jnp.transpose(send_ref[0]), -1)
+    targets = jnp.transpose(recv_ref[0])
+
+    def pick_rows(listed):
+        for q in range(parts):
+            column = listed[:, q : q + 1]
+            column = jnp.where(core == 0, column[:slots], column[slots:])
+            lane = lax.broadcasted_iota(jnp.int32, (slots, rows), 1)
+            own_pick[q * slots : (q + 1) * slots, :] = (column == lane).astype(f32).astype(bf16)
+
+    def lay_out(place, listed):
+        pieces = [
+            listed[h * slots : (h + 1) * slots, q : q + 1]
+            for h in range(2)
+            for q in range(parts)
+        ]
+        per = LANES // slots
+        for k in range(0, len(pieces), per):
+            column = jnp.concatenate(pieces[k : k + per], axis=0)
+            across = jnp.transpose(jnp.broadcast_to(column, (LANES, LANES)))
+            idx_ref[place : place + 1, k * slots : k * slots + LANES] = across[0:1, :]
+
+    pick_rows(sources)
     pl.semaphore_wait(barrier, parts)
 
     def halo_send(phase, onehot, source):
@@ -224,14 +253,20 @@
 
     weight_copies = []
     for k, (src, dst) in enumerate(((wg_in, wg), (wu_in, wu), (wd_in, wd))):
-        copy = remote(src, dst.at[core], w_send.at[k], w_recv.at[k], me, sib)
+        load_weights[k].wait()
+        copy = remote(dst.at[core], dst.at[core], w_send.at[k], w_recv.at[k], me, sib)
         copy.start()
         weight_copies.append(copy)
-        dst[core] = src[...]
+
+    load_tiles.wait()
+    lay_out(1, targets)
 
     def build(r, _):
+        held = [col_ref[r, j] for j in range(tiles_ref.shape[1])]
         for c in range(blocks):
-            j = inv_ref[r, c]
+            j = jnp.int32(-1)
+            for k, col in enumerate(held):
+                j = jnp.where(col == c, k, j)
             tile = tiles_ref[r, jnp.maximum(j, 0)]
             adj[aligned(r, BLOCK), c * BLOCK : (c + 1) * BLOCK] = jnp.where(
                 j >= 0, tile, jnp.zeros_like(tile)
@@ -251,13 +286,6 @@
         index = lax.broadcasted_iota(jnp.int32, (TILE, 2 * own_rows), 0) + i * TILE
         r_t[at, :] = (idx_ref[1:2, :] == index).astype(f32).astype(bf16)
         return 0
-
-    def build_back():
-        for begin in range(0, own_rows, step):
-            lane = lax.broadcasted_iota(jnp.int32, (step, rows), 1)
-            own_pick[begin : begin + step, :] = (own_cols[begin : begin + step, 1:2] == lane).astype(
-                f32
-            ).astype(bf16)
 
     def turn_tiles():
         def turn(r, _):
@@ -282,15 +310,21 @@
             for copy in weight_copies:
                 copy.wait_recv()
         if layer == layers - 1:
-            build_back()
+            pick_rows(targets)
+            lay_out(0, sources)
             each_tile(build_send)
             turn_tiles()
+            for plain, turned in ((wg, wg_t), (wu, wu_t), (wd, wd_t)):
+                for h in range(2):
+                    for k in range(layers):
+                        turned[h, k] = jnp.transpose(plain[h, k])
         halo_recv(layer)
 
         def mlp(i, _, layer=layer, state=state):
             at = aligned(i, TILE)
             act = (fg_ref[at, :] + dot_nn(r_t[at, :], landed_rows(layer))).astype(bf16)
-            acts[layer, at, :] = act
+            acts_t[layer, :, at] = jnp.transpose(act)
+            made = []
             mixed = jnp.zeros((TILE, width), f32)
             for h in range(2):
                 gate = dot_nn(act, wg[h, layer])
@@ -298,10 +332,11 @@
                 sg = 0.5 * jnp.tanh(0.5 * gate) + 0.5
                 silu = gate * sg
                 hidden = (silu * up).astype(bf16)
-                hid[layer, h, at, :] = hidden
+                made.append(hidden)
                 pre_g[layer, h, at, :] = (up * (sg * (1.0 + gate * (1.0 - sg)))).astype(bf16)
                 pre_u[layer, h, at, :] = silu.astype(bf16)
                 mixed = mixed + dot_nn(hidden, wd[h, layer])
+            hid_t[layer, :, at] = jnp.transpose(jnp.where(core == 0, made[0], made[1]))
             new = ((state[at, :].astype(f32) + mixed) * mask_of(i)).astype(bf16)
             if layer + 1 < layers:
                 states[layer + 1, at, :] = new
@@ -417,6 +452,16 @@
         own = at_rows(p_rows, z, q_seg)
         each_other(lambda t: line(3, layer, res.at[layer, own], res.at[layer, own], t, z).start())
 
+    def stores(layer):
+        return [
+            pltpu.make_async_copy(ref.at[layer], out.at[layer], o_sem.at[2 + k, layer])
+            for k, (ref, out) in enumerate(((gg_ref, gg_out), (gu_ref, gu_out), (gd_ref, gd_out)))
+        ]
+
+    store_final = pltpu.make_async_copy(final_ref, final_out, o_sem.at[0, 0])
+    store_final.start()
+    store_fg = pltpu.make_async_copy(fg_ref, fg_out, o_sem.at[1, 0])
+
     def reduce_end(layer):
         half = at_rows(0, 1 - y, p_half)
         pair(3, layer, res.at[layer, half], res.at[layer, half]).wait_recv()
@@ -427,11 +472,13 @@
 
         each_other(landed)
         at = 0
-        for out in (gg_out, gu_out, gd_out):
+        for out in (gg_ref, gu_ref, gd_ref):
             height, wide = out.shape[1:]
             for c in range(0, wide, LANES):
                 out[layer, :, c : c + LANES] = res[layer, at : at + height].astype(f32)
                 at += height
+        for copy in stores(layer):
+            copy.start()
 
     def reduce_drain(layer):
         pair(0, layer, grads.at[layer, at_rows(0, 1 - y, p_half)], p_one.at[layer]).wait_send()
@@ -462,6 +509,8 @@
 
     down_in, agg_grad = states.at[0], states.at[1]
 
+    load_cot.wait()
+
     def start_rows(i, _):
         at = aligned(i, TILE)
         fg_ref[at, :] = cot_ref[at, :].astype(f32) * mask_of(i)
@@ -478,7 +527,7 @@
             down = fg_ref[at, :].astype(bf16)
             down_in[at, :] = down
             for h in range(2):
-                hidden_grad = dot_nt(down, wd[h, layer])
+                hidden_grad = dot_nn(down, wd_t[h, layer])
                 gate_grad = (hidden_grad * pre_g[layer, h, at, :].astype(f32)).astype(bf16)
                 up_grad = (hidden_grad * pre_u[layer, h, at, :].astype(f32)).astype(bf16)
                 pre_g[layer, h, at, :] = gate_grad
@@ -489,20 +538,20 @@
             at = aligned(i, TILE)
             total = jnp.zeros((TILE, width), f32)
             for h in range(2):
-                total = total + dot_nt(pre_g[layer, h, at, :], wg[h, layer])
-                total = total + dot_nt(pre_u[layer, h, at, :], wu[h, layer])
+                total = total + dot_nn(pre_g[layer, h, at, :], wg_t[h, layer])
+                total = total + dot_nn(pre_u[layer, h, at, :], wu_t[h, layer])
             agg_grad[at, :] = total.astype(bf16)
             return 0
 
         def weight_gradients(layer=layer):
             at = 0
-            act = acts[layer]
+            act = acts_t[layer]
             for left, right in (
                 (act, pre_g[layer, core]),
                 (act, pre_u[layer, core]),
-                (hid[layer, core], down_in[...]),
+                (hid_t[layer], down_in[...]),
             ):
-                part = dot_tn(left, right).astype(bf16)
+                part = dot_nn(left, right).astype(bf16)
                 for c in range(0, part.shape[1], LANES):
                     grads[layer, at : at + part.shape[0], :] = part[:, c : c + LANES]
                     at += part.shape[0]
@@ -540,11 +589,16 @@
         else:
             reduce_end(layer + 1)
 
+    store_fg.start()
     reduce_three(0)
     reduce_four(0)
     reduce_end(0)
+    store_final.wait()
+    store_fg.wait()
     for layer in range(layers):
         reduce_drain(layer)
+        for copy in stores(layer):
+            copy.wait()
     for copy in weight_copies:
         copy.wait_send()
     for phase in range(2 * layers):
@@ -560,22 +614,28 @@
 
 
 def hand_over(*refs):
-    sems = refs[-1]
-    count = (len(refs) - 1) // 2
-    copies = []
+    count = (len(refs) - 2) // 3
+    in_sem, out_sem = refs[-2:]
+    pairs = []
     for k in range(count):
-        source, target = refs[k], refs[count + k]
+        source, target, held = refs[k], refs[count + k], refs[2 * count + k]
         cuts = 2 if source.shape[0] < 8 else 4
         size = source.shape[0] // cuts
         for cut in range(cuts):
             at = pl.ds(cut * size, size)
-            copies.append(
-                pltpu.make_async_copy(source.at[at], target.at[at], sems.at[k, cut])
+            pairs.append(
+                (
+                    pltpu.make_async_copy(source.at[at], held.at[at], in_sem.at[k, cut]),
+                    pltpu.make_async_copy(held.at[at], target.at[at], out_sem.at[k, cut]),
+                )
             )
-    for copy in copies:
-        copy.start()
-    for copy in copies:
-        copy.wait()
+    for load, _ in pairs:
+        load.start()
+    for load, store in pairs:
+        load.wait()
+        store.start()
+    for _, store in pairs:
+        store.wait()
 
 
 def local(
@@ -594,24 +654,16 @@
 ):
     rows, width = feats.shape
     layers, _, units = gate_weight_matrix.shape
-    blocks, per_row = tile_col.shape
     slot_count = send_list.shape[2]
     half = slot_count // 2
     outer = parts // 2
     all_slots = parts * slot_count
-    position = jnp.arange(1, per_row + 1, dtype=jnp.int32)[None, :, None]
-    chosen = tile_col[:, :, None] == jnp.arange(blocks, dtype=jnp.int32)[None, None, :]
-    inverse = jnp.sum(jnp.where(chosen, position, 0), axis=1) - 1
-    live = jnp.arange(slot_count)[None, :] < send_count[0][:, None]
-    listed = jnp.stack([jnp.where(live, send_list[0], -1), recv_list[0]])
-    listed = jnp.swapaxes(listed.reshape(2, parts, 2, half), 1, 2).reshape(2, all_slots)
-    listed = jnp.pad(listed, ((0, 6), (0, 0)))
-
     total = 2 * width * (units // LANES) + units * (width // LANES)
     p_half = total // 3
     q_seg = (total - 2 * p_half) // outer
     f32, bf16 = jnp.float32, jnp.bfloat16
     vmem = pl.BlockSpec(memory_space=pltpu.VMEM)
+    hbm = pl.BlockSpec(memory_space=pl.ANY)
     smem = pl.BlockSpec(memory_space=pltpu.SMEM)
     phases = 2 * layers
     dma = pltpu.SemaphoreType.DMA
@@ -624,22 +676,33 @@
             jax.ShapeDtypeStruct((layers, width, units), f32),
             jax.ShapeDtypeStruct((layers, units, width), f32),
         ),
-        in_specs=[smem, smem] + [vmem] * 7,
-        out_specs=[vmem] * 5,
+        in_specs=[smem, smem] + [vmem] * 4 + [hbm] * 5,
+        out_specs=[hbm] * 5,
         scratch_shapes=[
+            pltpu.VMEM((8, all_slots), jnp.int32),
+            pltpu.VMEM(tile_val.shape, bf16),
+            pltpu.VMEM((rows, width), bf16),
+            pltpu.VMEM((rows, width), bf16),
+            pltpu.VMEM((rows, width), f32),
+            pltpu.VMEM((layers, width, units), f32),
+            pltpu.VMEM((layers, width, units), f32),
+            pltpu.VMEM((layers, units, width), f32),
             pltpu.VMEM((rows, rows), bf16),
             pltpu.VMEM((rows, rows), bf16),
             pltpu.VMEM((all_slots // 2, rows), bf16),
             pltpu.VMEM((rows, all_slots), bf16),
             pltpu.VMEM((rows, all_slots), bf16),
             pltpu.VMEM((max(layers, 2), rows, width), bf16),
-            pltpu.VMEM((layers, rows, width), bf16),
-            pltpu.VMEM((layers, 2, rows, units), bf16),
+            pltpu.VMEM((layers, width, rows), bf16),
+            pltpu.VMEM((layers, units, rows), bf16),
             pltpu.VMEM((layers, 2, rows, units), bf16),
             pltpu.VMEM((layers, 2, rows, units), bf16),
             pltpu.VMEM((2, layers, width, units), bf16),
             pltpu.VMEM((2, layers, width, units), bf16),
             pltpu.VMEM((2, layers, units, width), bf16),
+            pltpu.VMEM((2, layers, units, width), bf16),
+            pltpu.VMEM((2, layers, units, width), bf16),
+            pltpu.VMEM((2, layers, width, units), bf16),
             pltpu.VMEM((phases, parts, half, width), bf16),
             pltpu.VMEM((phases, 2, parts, half, width), bf16),
             pltpu.VMEM((layers, total, LANES), bf16),
@@ -658,6 +721,8 @@
             dma((3,)),
             dma((layers, 4, outer + 1)),
             dma((layers, 4, outer + 1)),
+            dma((5,)),
+            dma((5, layers)),
         ],
         compiler_params=pltpu.CompilerParams(
             collective_id=0, has_side_effects=True, vmem_limit_bytes=60 * 1024 * 1024
@@ -666,9 +731,11 @@
             flops=14 * 10**9, bytes_accessed=12 * 10**6, transcendentals=rows * units * 4
         ),
     )(
-        inverse,
+        tile_col,
         cell_count,
-        listed,
+        send_list,
+        send_count,
+        recv_list,
         feats,
         tile_val,
         out_grad,
@@ -679,9 +746,11 @@
     return pl.pallas_call(
         hand_over,
         out_shape=tuple(jax.ShapeDtypeStruct(out.shape, out.dtype) for out in outs),
-        in_specs=[pl.BlockSpec(memory_space=pl.ANY)] * len(outs),
-        out_specs=[pl.BlockSpec(memory_space=pl.ANY)] * len(outs),
-        scratch_shapes=[dma((len(outs), 4))],
+        in_specs=[hbm] * len(outs),
+        out_specs=[hbm] * len(outs),
+        scratch_shapes=[pltpu.VMEM(out.shape, out.dtype) for out in outs]
+        + [dma((len(outs), 4)), dma((len(outs), 4))],
+        compiler_params=pltpu.CompilerParams(vmem_limit_bytes=60 * 1024 * 1024),
     )(*outs)
 
 

time: 197 us -> 75.7 us (0.38)
  Pallas kernels: 191 us -> 72.7 us
    pallas_call x1, Pallas kernels: 120 us -> 4.01 us  [local(): pl.pallas_call(hand_over, out_shape=tuple((jax.ShapeDtypeStruct(out.shape...]
    pallas_call x1, Pallas kernels: 70.8 us -> 68.7 us  [local(): pl.pallas_call(functools.partial(kernel, parts), out_shape=(jax.ShapeDtyp...]
where the time goes in v2:
time: 75.7 us; the launch traced here: 75.5 us
  Pallas kernels  72.7 us (96%)
  between operations  1.45 us (2%)
  local copies, waits for them, and re-layouts  1.36 us (2%)
    pallas_call x1, Pallas kernels, local(): pl.pallas_call(functools.partial(kernel, parts), out_shape=(jax.ShapeDtyp...  68.7 us
    pallas_call x1, Pallas kernels, local(): pl.pallas_call(hand_over, out_shape=tuple((jax.ShapeDtypeStruct(out.shape...  4.01 us

profile of v2, /device:TPU:0, one launch (start us, length us, event | category | flops | bytes accessed | tf_op | source)
XLA Modules:
  0.0 75.5 jit_solution(17313833678694210461)
XLA Ops:
  1.3 1.4 %copy.16.col_ref = s32[12,8]{1,0:T(8,128)} copy(s32[12,8]{0,1:T(8,128)} %param.13) | data formatting | bytes 768 | tf_op args[2]
  2.6 68.7 %shard_map.146 = (bf16[1536,256]{1,0:T(8,128)(2,1)}, f32[1536,256]{1,0:T(8,128)}, f32[2,256,256]{2,1,0:T(8,128)}, f32[2,256,256]{2,1,0:T(8,128)}, f32[2,256,256]{2,1,0:T(8,128)}) custom-call(s32[12,8]{1,0:T(8,128)} %copy.16.col_ref, s32[1]{0:T(128)S(6)} %copy.17.count_ref, s32[1,8,64]{2,1,0:T(8,128)} %send_ref.1, s32[1,8]{1,0:T(1,128)} %live_ref.1, ...), custom_call_target="tpu_custom_call" | custom-call | flops 14000000000 | bytes 12000000 | tf_op jit(solution)/shard_map/pallas_call | solution.py:670
  71.3 4.0 %shard_map.147 = (bf16[1536,256]{1,0:T(8,128)(2,1)}, f32[1536,256]{1,0:T(8,128)}, f32[2,256,256]{2,1,0:T(8,128)}, f32[2,256,256]{2,1,0:T(8,128)}, f32[2,256,256]{2,1,0:T(8,128)}) custom-call(bf16[1536,256]{1,0:T(8,128)(2,1)} %get-tuple-element.10.refs_0_, f32[1536,256]{1,0:T(8,128)} %get-tuple-element.11.refs_1_, f32[2,256,256]{2,1,0:T(8,128)} %get-tuple-element.12.refs_2_, ...), custom_call_target="tpu_custom_call" | custom-call | tf_op jit(solution)/shard_map/pallas_call | solution.py:746

commit v3 on v2

--- a/solution.py
+++ b/solution.py
@@ -262,7 +262,7 @@
     lay_out(1, targets)
 
     def build(r, _):
-        held = [col_ref[r, j] for j in range(tiles_ref.shape[1])]
+        held = [col_ref[j, r] for j in range(tiles_ref.shape[1])]
         for c in range(blocks):
             j = jnp.int32(-1)
             for k, col in enumerate(held):
@@ -363,94 +363,135 @@
 
         lax.fori_loop(1, outer, go, 0)
 
-    def pair(stage, layer, src, dst):
+    def pair(stage, layer, src, dst, slot):
         return remote(
             src,
             dst,
-            a_send.at[layer, stage, outer],
-            a_recv.at[layer, stage, outer],
+            a_send.at[layer, stage, outer + slot],
+            a_recv.at[layer, stage, outer + slot],
             z * 2 + 1 - y,
             core,
         )
 
-    def line(stage, layer, src, dst, to, slot):
+    def line(stage, layer, src, dst, to, slot, bank=0):
         return remote(
             src,
             dst,
-            a_send.at[layer, stage, to],
-            a_recv.at[layer, stage, slot],
+            a_send.at[layer, stage, bank * outer + to],
+            a_recv.at[layer, stage, bank * outer + slot],
             to * 2 + y,
             core,
         )
 
+    def p_first(layer, t):
+        return pair(
+            0,
+            layer,
+            grads.at[layer, at_rows((1 - y) * p_half, t, p_seg)],
+            p_one.at[layer, at_rows(0, t, p_seg)],
+            t,
+        )
+
+    def p_added(layer, t):
+        mine = grads[layer, at_rows(y * p_half, t, p_seg)].astype(f32)
+        return (mine + p_one[layer, at_rows(0, t, p_seg)].astype(f32)).astype(bf16)
+
+    def p_across(layer, t, slot):
+        return line(
+            1, layer, p_sum.at[layer, at_rows(0, t, p_seg)], p_two.at[layer, slot], t, slot
+        )
+
+    def p_spread(layer, owner, t, slot):
+        place = res.at[layer, at_rows(y * p_half, owner, p_seg)]
+        return line(2, layer, place, place, t, slot)
+
+    def p_last(layer, half, t):
+        place = res.at[layer, at_rows(half * p_half, t, p_seg)]
+        return pair(3, layer, place, place, t)
+
+    def q_first(layer, t, slot):
+        return line(
+            0,
+            layer,
+            grads.at[layer, at_rows(p_rows, t, q_seg)],
+            q_one.at[layer, slot],
+            t,
+            slot,
+        )
+
+    def q_across(layer):
+        source = q_sum.at[layer, at_rows(0, 1 - y, q_half)]
+        return pair(1, layer, source, q_two.at[layer], 0)
+
+    def q_spread(layer, half):
+        place = res.at[layer, at_rows(p_rows + z * q_seg, half, q_half)]
+        return pair(2, layer, place, place, 0)
+
+    def q_last(layer, owner, half, t, slot, bank):
+        place = res.at[layer, at_rows(p_rows + owner * q_seg, half, q_half)]
+        return line(3, layer, place, place, t, slot, 2 * bank)
+
     def reduce_one(layer):
-        pair(0, layer, grads.at[layer, at_rows(0, 1 - y, p_half)], p_one.at[layer]).start()
-        each_other(
-            lambda t: line(
-                0,
-                layer,
-                grads.at[layer, at_rows(p_rows, t, q_seg)],
-                q_one.at[layer, z],
-                t,
-                z,
-            ).start()
-        )
+        def send(t):
+            p_first(layer, t).start()
+            q_first(layer, t, z).start()
+
+        each_other(send)
+        p_first(layer, z).start()
         q_one[layer, z] = grads[layer, at_rows(p_rows, z, q_seg)]
 
     def reduce_two(layer):
-        pair(0, layer, grads.at[layer, at_rows(0, 1 - y, p_half)], p_one.at[layer]).wait_recv()
-        p_sum[layer] = (
-            grads[layer, at_rows(0, y, p_half)].astype(f32) + p_one[layer].astype(f32)
+        def pass_on(t):
+            p_first(layer, t).wait_recv()
+            p_sum[layer, at_rows(0, t, p_seg)] = p_added(layer, t)
+            p_across(layer, t, z).start()
+
+        each_other(pass_on)
+        p_first(layer, z).wait_recv()
+        p_two[layer, z] = p_added(layer, z)
+        each_other(lambda t: q_first(layer, t, t).wait_recv())
+        q_sum[layer] = jnp.sum(q_one[layer].astype(f32), axis=0).astype(bf16)
+        q_across(layer).start()
+
+    def reduce_three(layer):
+        each_other(lambda t: p_across(layer, t, t).wait_recv())
+        res[layer, at_rows(y * p_half, z, p_seg)] = jnp.sum(
+            p_two[layer].astype(f32), axis=0
         ).astype(bf16)
-        each_other(
-            lambda t: line(
-                1, layer, p_sum.at[layer, at_rows(0, t, p_seg)], p_two.at[layer, z], t, z
-            ).start()
-        )
-        p_two[layer, z] = p_sum[layer, at_rows(0, z, p_seg)]
-        each_other(
-            lambda t: line(
-                0,
-                layer,
-                grads.at[layer, at_rows(p_rows, t, q_seg)],
-                q_one.at[layer, t],
-                t,
-                t,
-            ).wait_recv()
-        )
-        q_sum[layer] = jnp.sum(q_one[layer].astype(f32), axis=0).astype(bf16)
-        pair(1, layer, q_sum.at[layer, at_rows(0, 1 - y, q_half)], q_two.at[layer]).start()
-
-    def reduce_three(layer):
-        each_other(
-            lambda t: line(
-                1, layer, p_sum.at[layer, at_rows(0, t, p_seg)], p_two.at[layer, t], t, t
-            ).wait_recv()
-        )
-        mine = at_rows(y * p_half, z, p_seg)
-        res[layer, mine] = jnp.sum(p_two[layer].astype(f32), axis=0).astype(bf16)
-        each_other(
-            lambda t: line(2, layer, res.at[layer, mine], res.at[layer, mine], t, z).start()
-        )
-        pair(1, layer, q_sum.at[layer, at_rows(0, 1 - y, q_half)], q_two.at[layer]).wait_recv()
-        own = at_rows(p_rows + z * q_seg, y, q_half)
-        res[layer, own] = (
+        each_other(lambda t: p_spread(layer, z, t, z).start())
+        p_last(layer, y, z).start()
+        q_across(layer).wait_recv()
+        res[layer, at_rows(p_rows + z * q_seg, y, q_half)] = (
             q_sum[layer, at_rows(0, y, q_half)].astype(f32) + q_two[layer].astype(f32)
         ).astype(bf16)
-        pair(2, layer, res.at[layer, own], res.at[layer, own]).start()
+        q_spread(layer, y).start()
+        each_other(lambda t: q_last(layer, z, y, t, z, 0).start())
 
     def reduce_four(layer):
-        def landed(t):
-            there = at_rows(y * p_half, t, p_seg)
-            line(2, layer, res.at[layer, there], res.at[layer, there], t, t).wait_recv()
-
-        each_other(landed)
-        half = at_rows(0, y, p_half)
-        pair(3, layer, res.at[layer, half], res.at[layer, half]).start()
-        other = at_rows(p_rows + z * q_seg, 1 - y, q_half)
-        pair(2, layer, res.at[layer, other], res.at[layer, other]).wait_recv()
-        own = at_rows(p_rows, z, q_seg)
-        each_other(lambda t: line(3, layer, res.at[layer, own], res.at[layer, own], t, z).start())
+        q_spread(layer, 1 - y).wait_recv()
+
+        def pass_on(t):
+            p_spread(layer, t, t, t).wait_recv()
+            p_last(layer, y, t).start()
+            q_last(layer, z, 1 - y, t, z, 1).start()
+
+        each_other(pass_on)
+
+    def reduce_drain(layer):
+        def sent(t):
+            p_first(layer, t).wait_send()
+            q_first(layer, t, z).wait_send()
+            p_across(layer, t, z).wait_send()
+            p_spread(layer, z, t, z).wait_send()
+            p_last(layer, y, t).wait_send()
+            q_last(layer, z, y, t, z, 0).wait_send()
+            q_last(layer, z, 1 - y, t, z, 1).wait_send()
+
+        each_other(sent)
+        p_first(layer, z).wait_send()
+        p_last(layer, y, z).wait_send()
+        q_across(layer).wait_send()
+        q_spread(layer, y).wait_send()
 
     def stores(layer):
         return [
@@ -463,14 +504,13 @@
     store_fg = pltpu.make_async_copy(fg_ref, fg_out, o_sem.at[1, 0])
 
     def reduce_end(layer):
-        half = at_rows(0, 1 - y, p_half)
-        pair(3, layer, res.at[layer, half], res.at[layer, half]).wait_recv()
-
         def landed(t):
-            there = at_rows(p_rows, t, q_seg)
-            line(3, layer, res.at[layer, there], res.at[layer, there], t, t).wait_recv()
+            p_last(layer, 1 - y, t).wait_recv()
+            q_last(layer, t, y, t, t, 0).wait_recv()
+            q_last(layer, t, 1 - y, t, t, 1).wait_recv()
 
         each_other(landed)
+        p_last(layer, 1 - y, z).wait_recv()
         at = 0
         for out in (gg_ref, gu_ref, gd_ref):
             height, wide = out.shape[1:]
@@ -480,35 +520,7 @@
         for copy in stores(layer):
             copy.start()
 
-    def reduce_drain(layer):
-        pair(0, layer, grads.at[layer, at_rows(0, 1 - y, p_half)], p_one.at[layer]).wait_send()
-        pair(1, layer, q_sum.at[layer, at_rows(0, 1 - y, q_half)], q_two.at[layer]).wait_send()
-        own = at_rows(p_rows + z * q_seg, y, q_half)
-        pair(2, layer, res.at[layer, own], res.at[layer, own]).wait_send()
-        half = at_rows(0, y, p_half)
-        pair(3, layer, res.at[layer, half], res.at[layer, half]).wait_send()
-        mine = at_rows(y * p_half, z, p_seg)
-        whole = at_rows(p_rows, z, q_seg)
-
-        def sent(t):
-            line(
-                0,
-                layer,
-                grads.at[layer, at_rows(p_rows, t, q_seg)],
-                q_one.at[layer, z],
-                t,
-                z,
-            ).wait_send()
-            line(
-                1, layer, p_sum.at[layer, at_rows(0, t, p_seg)], p_two.at[layer, z], t, z
-            ).wait_send()
-            line(2, layer, res.at[layer, mine], res.at[layer, mine], t, z).wait_send()
-            line(3, layer, res.at[layer, whole], res.at[layer, whole], t, z).wait_send()
-
-        each_other(sent)
-
     down_in, agg_grad = states.at[0], states.at[1]
-
     load_cot.wait()
 
     def start_rows(i, _):
@@ -559,17 +571,15 @@
 
         each_tile(mlp_back)
         if layer == 0:
+            weight_gradients()
             if not last:
                 reduce_three(layer + 1)
-            weight_gradients()
         each_tile(through_weights)
         halo_send(phase, own_pick, agg_grad)
         if layer:
             if not last:
                 reduce_three(layer + 1)
             weight_gradients()
-        if not last:
-            reduce_four(layer + 1)
 
         for begin in range(0, rows, 2 * TILE):
             at = pl.ds(begin, 2 * TILE)
@@ -577,6 +587,8 @@
         if not last:
             reduce_two(layer)
         halo_recv(phase)
+        if not last:
+            reduce_four(layer + 1)
 
         def finish(i, _, phase=phase):
             at = aligned(i, TILE)
@@ -586,11 +598,11 @@
         each_tile(finish)
         if last:
             reduce_two(layer)
-        else:
-            reduce_end(layer + 1)
 
     store_fg.start()
     reduce_three(0)
+    for layer in range(1, layers):
+        reduce_end(layer)
     reduce_four(0)
     reduce_end(0)
     store_final.wait()
@@ -719,8 +731,8 @@
             dma((phases, parts)),
             dma((3,)),
             dma((3,)),
-            dma((layers, 4, outer + 1)),
-            dma((layers, 4, outer + 1)),
+            dma((layers, 4, 3 * outer)),
+            dma((layers, 4, 3 * outer)),
             dma((5,)),
             dma((5, layers)),
         ],
@@ -731,7 +743,7 @@
             flops=14 * 10**9, bytes_accessed=12 * 10**6, transcendentals=rows * units * 4
         ),
     )(
-        tile_col,
+        jnp.transpose(tile_col),
         cell_count,
         send_list,
         send_count,

time: 75.7 us -> 72.6 us (0.959)
  Pallas kernels: 72.7 us -> 70.9 us
  local copies, waits for them, and re-layouts: 1.36 us -> 0 us
    pallas_call x1, Pallas kernels: 68.7 us -> 66.9 us  [local(): pl.pallas_call(functools.partial(kernel, parts), out_shape=(jax.ShapeDtyp...]
    unnamed x1 -> x0, local copies, waits for them, and re-layouts: 1.36 us -> none
where the time goes in v3:
time: 72.6 us; the launch traced here: 72.4 us
  Pallas kernels  70.9 us (98%)
  between operations  1.45 us (2%)
    pallas_call x1, Pallas kernels, local(): pl.pallas_call(functools.partial(kernel, parts), out_shape=(jax.ShapeDtyp...  66.9 us
    pallas_call x1, Pallas kernels, local(): pl.pallas_call(hand_over, out_shape=tuple((jax.ShapeDtypeStruct(out.shape...  4.01 us

profile of v3, /device:TPU:0, one launch (start us, length us, event | category | flops | bytes accessed | tf_op | source)
XLA Modules:
  0.0 72.4 jit_solution(11324499907452803384)
XLA Ops:
  1.3 66.9 %shard_map.146 = (bf16[1536,256]{1,0:T(8,128)(2,1)}, f32[1536,256]{1,0:T(8,128)}, f32[2,256,256]{2,1,0:T(8,128)}, f32[2,256,256]{2,1,0:T(8,128)}, f32[2,256,256]{2,1,0:T(8,128)}) custom-call(s32[8,12]{1,0:T(8,128)} %bitcast.1, s32[1]{0:T(128)S(6)} %copy.16.count_ref, s32[1,8,64]{2,1,0:T(8,128)} %send_ref.1, s32[1,8]{1,0:T(1,128)} %live_ref.1, ...), custom_call_target="tpu_custom_call" | custom-call | flops 14000000000 | bytes 12000000 | tf_op jit(solution)/shard_map/pallas_call | solution.py:682
  68.2 4.0 %shard_map.147 = (bf16[1536,256]{1,0:T(8,128)(2,1)}, f32[1536,256]{1,0:T(8,128)}, f32[2,256,256]{2,1,0:T(8,128)}, f32[2,256,256]{2,1,0:T(8,128)}, f32[2,256,256]{2,1,0:T(8,128)}) custom-call(bf16[1536,256]{1,0:T(8,128)(2,1)} %get-tuple-element.10.refs_0_, f32[1536,256]{1,0:T(8,128)} %get-tuple-element.11.refs_1_, f32[2,256,256]{2,1,0:T(8,128)} %get-tuple-element.12.refs_2_, ...), custom_call_target="tpu_custom_call" | custom-call | tf_op jit(solution)/shard_map/pallas_call | solution.py:758

commit v4 on v3

--- a/solution.py
+++ b/solution.py
@@ -98,6 +98,7 @@
     a_recv,
     i_sem,
     o_sem,
+    inv_ref,
 ):
     me = lax.axis_index("dom")
     core = lax.axis_index("mp")
@@ -179,9 +180,7 @@
             idx_ref[place : place + 1, k * slots : k * slots + LANES] = across[0:1, :]
 
     pick_rows(sources)
-    pl.semaphore_wait(barrier, parts)
-
-    def halo_send(phase, onehot, source):
+    def halo_pick(phase, onehot, source):
         for begin in range(0, own_rows, step):
             picked = dot_nn(onehot[begin : begin + step, :], source[...]).astype(bf16)
             sbuf[phase, begin // slots : (begin + step) // slots] = picked.reshape(
@@ -189,6 +188,7 @@
             )
         halo[phase, core, me] = sbuf[phase, me]
 
+    def halo_send(phase):
         def send(i, _):
             q = lax.rem(me + i, parts)
             remote(
@@ -249,7 +249,9 @@
     def landed_rows(phase):
         return halo[phase].reshape(2 * own_rows, width)
 
-    halo_send(0, own_pick, states.at[0])
+    halo_pick(0, own_pick, states.at[0])
+    pl.semaphore_wait(barrier, parts)
+    halo_send(0)
 
     weight_copies = []
     for k, (src, dst) in enumerate(((wg_in, wg), (wu_in, wu), (wd_in, wd))):
@@ -267,6 +269,7 @@
             j = jnp.int32(-1)
             for k, col in enumerate(held):
                 j = jnp.where(col == c, k, j)
+            inv_ref[r, c] = j
             tile = tiles_ref[r, jnp.maximum(j, 0)]
             adj[aligned(r, BLOCK), c * BLOCK : (c + 1) * BLOCK] = jnp.where(
                 j >= 0, tile, jnp.zeros_like(tile)
@@ -287,19 +290,27 @@
         r_t[at, :] = (idx_ref[1:2, :] == index).astype(f32).astype(bf16)
         return 0
 
-    def turn_tiles():
+    def place_turned():
         def turn(r, _):
             for c in range(blocks):
-                adj_t[c * BLOCK : (c + 1) * BLOCK, aligned(r, BLOCK)] = jnp.transpose(
-                    adj[aligned(r, BLOCK), c * BLOCK : (c + 1) * BLOCK]
+                j = inv_ref[r, c]
+                tile = tiles_ref[r, jnp.maximum(j, 0)]
+                adj_t[c * BLOCK : (c + 1) * BLOCK, aligned(r, BLOCK)] = jnp.where(
+                    j >= 0, tile, jnp.zeros_like(tile)
                 )
             return 0
 
         lax.fori_loop(0, blocks, turn, 0)
+
+    def turn_share(part, whole):
+        for r in range(part * blocks // whole, (part + 1) * blocks // whole):
+            for j in range(tiles_ref.shape[1]):
+                tiles_ref[r, j] = jnp.transpose(tiles_ref[r, j])
 
     for layer in range(layers):
         if layer:
-            halo_send(layer, own_pick, states.at[layer])
+            halo_pick(layer, own_pick, states.at[layer])
+            halo_send(layer)
         state = states.at[layer]
 
         for begin in range(0, rows, 2 * TILE):
@@ -313,7 +324,6 @@
             pick_rows(targets)
             lay_out(0, sources)
             each_tile(build_send)
-            turn_tiles()
             for plain, turned in ((wg, wg_t), (wu, wu_t), (wd, wd_t)):
                 for h in range(2):
                     for k in range(layers):
@@ -322,6 +332,7 @@
 
         def mlp(i, _, layer=layer, state=state):
             at = aligned(i, TILE)
+            turn_share(layer * tiles + i, layers * tiles)
             act = (fg_ref[at, :] + dot_nn(r_t[at, :], landed_rows(layer))).astype(bf16)
             acts_t[layer, :, at] = jnp.transpose(act)
             made = []
@@ -575,11 +586,14 @@
             if not last:
                 reduce_three(layer + 1)
         each_tile(through_weights)
-        halo_send(phase, own_pick, agg_grad)
+        halo_pick(phase, own_pick, agg_grad)
+        halo_send(phase)
         if layer:
             if not last:
                 reduce_three(layer + 1)
             weight_gradients()
+        if last:
+            place_turned()
 
         for begin in range(0, rows, 2 * TILE):
             at = pl.ds(begin, 2 * TILE)
@@ -688,7 +702,7 @@
             jax.ShapeDtypeStruct((layers, width, units), f32),
             jax.ShapeDtypeStruct((layers, units, width), f32),
         ),
-        in_specs=[smem, smem] + [vmem] * 4 + [hbm] * 5,
+        in_specs=[smem, smem] + [vmem] * 4 + [pl.BlockSpec(memory_space=pltpu.HBM)] * 5,
         out_specs=[hbm] * 5,
         scratch_shapes=[
             pltpu.VMEM((8, all_slots), jnp.int32),
@@ -735,9 +749,10 @@
             dma((layers, 4, 3 * outer)),
             dma((5,)),
             dma((5, layers)),
+            pltpu.SMEM((rows // BLOCK, rows // BLOCK), jnp.int32),
         ],
         compiler_params=pltpu.CompilerParams(
-            collective_id=0, has_side_effects=True, vmem_limit_bytes=60 * 1024 * 1024
+            collective_id=0, has_side_effects=True, vmem_limit_bytes=min(60, 44 + parts // 2) * 1024 * 1024
         ),
         cost_estimate=pl.CostEstimate(
             flops=14 * 10**9, bytes_accessed=12 * 10**6, transcendentals=rows * units * 4
@@ -762,7 +777,7 @@
         out_specs=[hbm] * len(outs),
         scratch_shapes=[pltpu.VMEM(out.shape, out.dtype) for out in outs]
         + [dma((len(outs), 4)), dma((len(outs), 4))],
-        compiler_params=pltpu.CompilerParams(vmem_limit_bytes=60 * 1024 * 1024),
+        compiler_params=pltpu.CompilerParams(vmem_limit_bytes=8 * 1024 * 1024),
     )(*outs)
 
 

time: 72.6 us -> 80.6 us (1.11)
  local copies, waits for them, and re-layouts: 0 us -> 9.22 us
  Pallas kernels: 70.9 us -> 69.4 us
    unnamed x0 -> x20, local copies, waits for them, and re-layouts: none -> 9.22 us
    pallas_call x1, Pallas kernels: 66.9 us -> 65.3 us  [local(): pl.pallas_call(functools.partial(kernel, parts), out_shape=(jax.ShapeDtyp...]
where the time goes in v4:
time: 80.6 us; the launch traced here: 80.1 us
  Pallas kernels  69.4 us (86%)
  local copies, waits for them, and re-layouts  9.22 us (11%)
  between operations  1.47 us (2%)
    pallas_call x1, Pallas kernels, local(): pl.pallas_call(functools.partial(kernel, parts), out_shape=(jax.ShapeDtyp...  65.3 us
    unnamed x20, local copies, waits for them, and re-layouts  9.22 us
    pallas_call x1, Pallas kernels, local(): pl.pallas_call(hand_over, out_shape=tuple((jax.ShapeDtypeStruct(out.shape...  4.09 us

profile of v4, /device:TPU:0, one launch (start us, length us, event | category | flops | bytes accessed | tf_op | source)
XLA Modules:
  0.0 80.1 jit_solution(10489175647990750421)
XLA Ops:
  1.3 0.0 copy-start.1
  1.3 1.1 %copy-done.1 = bf16[1536,256]{1,0:T(8,128)(2,1)S(1)} copy-done((bf16[1536,256]{1,0:T(8,128)(2,1)S(1)}, bf16[1536,256]{1,0:T(8,128)(2,1)}, u32[]{:S(2)}) %copy-start.1) | copy-done | bytes 786456
  2.4 0.0 copy-start.2
  2.4 1.1 %copy-done.2 = bf16[1536,256]{1,0:T(8,128)(2,1)S(1)} copy-done((bf16[1536,256]{1,0:T(8,128)(2,1)S(1)}, bf16[1536,256]{1,0:T(8,128)(2,1)}, u32[]{:S(2)}) %copy-start.2) | copy-done | bytes 786456
  3.5 0.0 copy-start.3
  3.6 0.9 %copy-done.3 = bf16[2,256,256]{2,1,0:T(8,128)(2,1)S(1)} copy-done((bf16[2,256,256]{2,1,0:T(8,128)(2,1)S(1)}, bf16[2,256,256]{2,1,0:T(8,128)(2,1)}, u32[]{:S(2)}) %copy-start.3) | copy-done | bytes 262168
  4.5 0.0 copy-start.4
  4.5 0.9 %copy-done.4 = bf16[2,256,256]{2,1,0:T(8,128)(2,1)S(1)} copy-done((bf16[2,256,256]{2,1,0:T(8,128)(2,1)S(1)}, bf16[2,256,256]{2,1,0:T(8,128)(2,1)}, u32[]{:S(2)}) %copy-start.4) | copy-done | bytes 262168
  5.5 0.0 copy-start.5
  5.5 0.9 %copy-done.5 = bf16[2,256,256]{2,1,0:T(8,128)(2,1)S(1)} copy-done((bf16[2,256,256]{2,1,0:T(8,128)(2,1)S(1)}, bf16[2,256,256]{2,1,0:T(8,128)(2,1)}, u32[]{:S(2)}) %copy-start.5) | copy-done | bytes 262168
  6.4 0.0 copy-start.6
  6.4 0.7 copy-done.6
  7.1 0.0 copy-start.7
  7.1 0.7 copy-done.7
  7.8 0.0 copy-start.8
  7.8 0.7 copy-done.8
  8.5 0.0 copy-start.9
  8.5 0.7 copy-done.9
  9.1 65.3 %shard_map.146 = (bf16[1536,256]{1,0:T(8,128)(2,1)S(1)}, f32[1536,256]{1,0:T(8,128)}, f32[2,256,256]{2,1,0:T(8,128)S(1)}, f32[2,256,256]{2,1,0:T(8,128)S(1)}, f32[2,256,256]{2,1,0:T(8,128)S(1)}) custom-call(s32[8,12]{1,0:T(8,128)S(1)} %bitcast.1, s32[1]{0:T(128)S(6)} %copy.16.count_ref, s32[1,8,64]{2,1,0:T(8,128)S(1)} %copy-done.7, s32[1,8]{1,0:T(1,128)S(1)} %copy-done.9, ...), custom_call_target="tpu_custom_call" | custom-call | flops 14000000000 | bytes 12000000 | tf_op jit(solution)/shard_map/pallas_call | solution.py:696
  74.5 0.0 copy-start
  74.5 1.4 %copy-done = f32[1536,256]{1,0:T(8,128)S(1)} copy-done((f32[1536,256]{1,0:T(8,128)S(1)}, f32[1536,256]{1,0:T(8,128)}, u32[]{:S(2)}) %copy-start) | copy-done | bytes 1572888
  75.9 4.1 %shard_map.147 = (bf16[1536,256]{1,0:T(8,128)(2,1)}, f32[1536,256]{1,0:T(8,128)}, f32[2,256,256]{2,1,0:T(8,128)}, f32[2,256,256]{2,1,0:T(8,128)}, f32[2,256,256]{2,1,0:T(8,128)}) custom-call(bf16[1536,256]{1,0:T(8,128)(2,1)S(1)} %get-tuple-element.10.refs_0_, f32[1536,256]{1,0:T(8,128)S(1)} %copy-done, f32[2,256,256]{2,1,0:T(8,128)S(1)} %get-tuple-element.12.refs_2_, ...), custom_call_target="tpu_custom_call" | custom-call | tf_op jit(solution)/shard_map/pallas_call | solution.py:773
Async XLA Ops:
  1.3 1.1 %copy-start.1 = (bf16[1536,256]{1,0:T(8,128)(2,1)S(1)}, bf16[1536,256]{1,0:T(8,128)(2,1)}, u32[]{:S(2)}) copy-start(bf16[1536,256]{1,0:T(8,128)(2,1)} %feats_ref.1) | copy-start | bytes 2359300
  2.4 1.1 %copy-start.2 = (bf16[1536,256]{1,0:T(8,128)(2,1)S(1)}, bf16[1536,256]{1,0:T(8,128)(2,1)}, u32[]{:S(2)}) copy-start(bf16[1536,256]{1,0:T(8,128)(2,1)} %cot_in.1) | copy-start | bytes 2359300
  3.5 0.9 %copy-start.3 = (bf16[2,256,256]{2,1,0:T(8,128)(2,1)S(1)}, bf16[2,256,256]{2,1,0:T(8,128)(2,1)}, u32[]{:S(2)}) copy-start(bf16[2,256,256]{2,1,0:T(8,128)(2,1)} %wg_in.1) | copy-start | bytes 786436
  4.5 0.9 %copy-start.4 = (bf16[2,256,256]{2,1,0:T(8,128)(2,1)S(1)}, bf16[2,256,256]{2,1,0:T(8,128)(2,1)}, u32[]{:S(2)}) copy-start(bf16[2,256,256]{2,1,0:T(8,128)(2,1)} %wu_in.1) | copy-start | bytes 786436
  5.5 0.9 %copy-start.5 = (bf16[2,256,256]{2,1,0:T(8,128)(2,1)S(1)}, bf16[2,256,256]{2,1,0:T(8,128)(2,1)}, u32[]{:S(2)}) copy-start(bf16[2,256,256]{2,1,0:T(8,128)(2,1)} %wd_in.1) | copy-start | bytes 786436
  6.4 0.7 copy-start.6
  7.1 0.7 copy-start.7
  7.8 0.7 copy-start.8
  8.5 0.7 copy-start.9
  74.5 1.4 %copy-start = (f32[1536,256]{1,0:T(8,128)S(1)}, f32[1536,256]{1,0:T(8,128)}, u32[]{:S(2)}) copy-start(f32[1536,256]{1,0:T(8,128)} %get-tuple-element.11.refs_1_) | copy-start | bytes 4718596

commit v5 on v4

--- a/solution.py
+++ b/solution.py
@@ -702,7 +702,7 @@
             jax.ShapeDtypeStruct((layers, width, units), f32),
             jax.ShapeDtypeStruct((layers, units, width), f32),
         ),
-        in_specs=[smem, smem] + [vmem] * 4 + [pl.BlockSpec(memory_space=pltpu.HBM)] * 5,
+        in_specs=[smem, smem] + [vmem] * 4 + [hbm] * 5,
         out_specs=[hbm] * 5,
         scratch_shapes=[
             pltpu.VMEM((8, all_slots), jnp.int32),
@@ -752,7 +752,7 @@
             pltpu.SMEM((rows // BLOCK, rows // BLOCK), jnp.int32),
         ],
         compiler_params=pltpu.CompilerParams(
-            collective_id=0, has_side_effects=True, vmem_limit_bytes=min(60, 44 + parts // 2) * 1024 * 1024
+            collective_id=0, has_side_effects=True, vmem_limit_bytes=60 * 1024 * 1024
         ),
         cost_estimate=pl.CostEstimate(
             flops=14 * 10**9, bytes_accessed=12 * 10**6, transcendentals=rows * units * 4
@@ -777,7 +777,7 @@
         out_specs=[hbm] * len(outs),
         scratch_shapes=[pltpu.VMEM(out.shape, out.dtype) for out in outs]
         + [dma((len(outs), 4)), dma((len(outs), 4))],
-        compiler_params=pltpu.CompilerParams(vmem_limit_bytes=8 * 1024 * 1024),
+        compiler_params=pltpu.CompilerParams(vmem_limit_bytes=60 * 1024 * 1024),
     )(*outs)
 
 

time: 80.6 us -> 72.1 us (0.89)
  local copies, waits for them, and re-layouts: 9.22 us -> 0 us
  Pallas kernels: 69.4 us -> 70.5 us
    unnamed x20 -> x0, local copies, waits for them, and re-layouts: 9.22 us -> none
    pallas_call x1, Pallas kernels: 65.3 us -> 66.5 us  [local(): pl.pallas_call(functools.partial(kernel, parts), out_shape=(jax.ShapeDtyp...]
where the time goes in v5:
time: 72.1 us; the launch traced here: 72 us
  Pallas kernels  70.5 us (98%)
  between operations  1.45 us (2%)
    pallas_call x1, Pallas kernels, local(): pl.pallas_call(functools.partial(kernel, parts), out_shape=(jax.ShapeDtyp...  66.5 us
    pallas_call x1, Pallas kernels, local(): pl.pallas_call(hand_over, out_shape=tuple((jax.ShapeDtypeStruct(out.shape...  4.01 us

profile of v5, /device:TPU:0, one launch (start us, length us, event | category | flops | bytes accessed | tf_op | source)
XLA Modules:
  0.0 72.0 jit_solution(12595355393062327904)
XLA Ops:
  1.3 66.5 %shard_map.146 = (bf16[1536,256]{1,0:T(8,128)(2,1)}, f32[1536,256]{1,0:T(8,128)}, f32[2,256,256]{2,1,0:T(8,128)}, f32[2,256,256]{2,1,0:T(8,128)}, f32[2,256,256]{2,1,0:T(8,128)}) custom-call(s32[8,12]{1,0:T(8,128)} %bitcast.1, s32[1]{0:T(128)S(6)} %copy.16.count_ref, s32[1,8,64]{2,1,0:T(8,128)} %send_ref.1, s32[1,8]{1,0:T(1,128)} %live_ref.1, ...), custom_call_target="tpu_custom_call" | custom-call | flops 14000000000 | bytes 12000000 | tf_op jit(solution)/shard_map/pallas_call | solution.py:696
  67.8 4.0 %shard_map.147 = (bf16[1536,256]{1,0:T(8,128)(2,1)}, f32[1536,256]{1,0:T(8,128)}, f32[2,256,256]{2,1,0:T(8,128)}, f32[2,256,256]{2,1,0:T(8,128)}, f32[2,256,256]{2,1,0:T(8,128)}) custom-call(bf16[1536,256]{1,0:T(8,128)(2,1)} %get-tuple-element.10.refs_0_, f32[1536,256]{1,0:T(8,128)} %get-tuple-element.11.refs_1_, f32[2,256,256]{2,1,0:T(8,128)} %get-tuple-element.12.refs_2_, ...), custom_call_target="tpu_custom_call" | custom-call | tf_op jit(solution)/shard_map/pallas_call | solution.py:773
